TPU v7x, 512 devices: a whole 4x8x8 slice. The times are simulated.
512 devices in a mesh: role: 4 (over x), ep: 64 (over z, y), dp: 2 (over core).
Axes of the slice: x: 4, y: 8, z: 8, core: 2. Of those that a mesh axis runs over, the one named last changes fastest.
Arguments:
- latents: bfloat16 [16, 4096, 1536], P(('role', 'dp'), 'ep'), may hold values from -6 to 6
- noise: bfloat16 [1, 16, 4096, 1536], P(None, ('role', 'dp'), 'ep'), may hold values from -6 to 6
- expert_ids: int32 [1, 16, 4096, 6], P(None, ('role', 'dp'), 'ep'), may hold values from 0 to 63, all different within a row; in each aligned block of 64 rows (0 to 63, 64 to 127, ..., all dimensions but the last counted through in order) at most 7 rows name the same one
- gate_values: float32 [1, 16, 4096, 6], P(None, ('role', 'dp'), 'ep'), may hold values from 0.1 to 1
- advantages: float32 [16], P(('role', 'dp')), may hold values from -4 to 4
- expert_pair: bfloat16 [64, 2, 768, 1536], P('ep', None, ('role', 'dp')), may hold values from -6 to 6
Outputs:
- final_latents: bfloat16 [16, 4096, 1536], P(('role', 'dp'), 'ep')
- new_down: bfloat16 [64, 768, 1536], P('ep')
Inputs may be any that keep to these rules, and one draw needn't show every extreme that they name: `expert_ids`: each row names 6 different experts. In every aligned block of 64 rows (steps, images and tokens taken together in order; one index of ep holds one block of an image at a step) no expert is named more than 7 times, a bound that some block reaches.
All inputs are finite; a program needn't handle non-finite values.
Results may differ from a plain program's by a relative error of at most 0.008.
Values may be sent and summed in bfloat16 or wider, within the bound.
A program may use at most 128 MiB of HBM per device.

v0:
```python
import math

import jax
import jax.numpy as jnp
from jax import lax
from jax.sharding import PartitionSpec as P

CAP = 7


def coefficients(section):
    moment = 0.95 - 0.4 * section
    noise_level = 0.3 * math.sqrt(moment / (1.0 - moment))
    factor = noise_level * noise_level / (2.0 * moment)
    keep_gain = 1.0 - 0.4 * factor
    drift_gain = -0.4 * (1.0 + factor * (1.0 - moment))
    noise_gain = noise_level * math.sqrt(0.4)
    return (keep_gain, drift_gain, noise_gain)


def slot_matrices(picked, weights, experts, capacity):
    image_count, tokens, chosen_count = picked.shape
    flat_ids = picked.reshape(image_count, tokens * chosen_count)
    onehot = (flat_ids[..., None] == jnp.arange(experts, dtype=jnp.int32)).astype(jnp.int32)
    ranks = jnp.cumsum(onehot, axis=1) - 1
    placed = jnp.sum(ranks * onehot, axis=2)
    image_column = jnp.arange(image_count, dtype=jnp.int32)[:, None]
    slot_ids = (flat_ids * image_count + image_column) * capacity + placed
    slot_ids = slot_ids.reshape(image_count * tokens, chosen_count)
    total_slots = experts * image_count * capacity
    marked = (slot_ids[..., None] == jnp.arange(total_slots, dtype=jnp.int32)).astype(jnp.float32)
    selected = jnp.sum(marked, axis=1)
    flat_weights = weights.reshape(image_count * tokens, chosen_count)
    slot_gate = jnp.sum(jnp.sum(marked * flat_weights[..., None], axis=1), axis=0)
    return (slot_ids, selected, slot_gate, flat_weights)


def expert_pass(inputs, w_up, w_down):
    width = inputs.shape[-1]
    hidden_units = w_up.shape[1]
    pre_act = jnp.einsum("jlcd,lhd->jlch", inputs, w_up, preferred_element_type=jnp.float32) * (
        1.0 / math.sqrt(width)
    )
    hidden = jax.nn.gelu(pre_act, approximate=True).astype(jnp.bfloat16)
    output = jnp.einsum("jlch,lhd->jlcd", hidden, w_down, preferred_element_type=jnp.float32) * (
        1.0 / math.sqrt(hidden_units)
    )
    returned = lax.all_to_all(
        output.astype(jnp.bfloat16), "ep", split_axis=0, concat_axis=0, tiled=True
    )
    return (returned, hidden)


def per_device(latents, noise, expert_ids, gate_values, advantages, expert_pair):
    ep_size = lax.axis_size("ep")
    group_size = lax.axis_size("role") * lax.axis_size("dp")
    local_experts = expert_pair.shape[0]
    experts = local_experts * ep_size
    capacity = CAP
    image_count = latents.shape[0]
    tok_count = latents.shape[1]
    width = latents.shape[2]
    top_count = expert_ids.shape[3]
    total_slots = experts * image_count * capacity
    full_pair = lax.all_gather(expert_pair, ("role", "dp"), axis=2, tiled=True)
    w_up = full_pair[:, 0]
    w_down = full_pair[:, 1]
    hidden_units = full_pair.shape[2]
    current = latents.reshape(image_count * tok_count, width)
    image_of_slot = jnp.arange(total_slots, dtype=jnp.int32) // capacity % image_count
    keep_gain, drift_gain, noise_gain = coefficients(0)
    slot_ids, selected, slot_gate, flat_weights = slot_matrices(
        expert_ids[0], gate_values[0], experts, capacity
    )
    selected_half = selected.astype(jnp.bfloat16)
    noise_now = noise[0].reshape(image_count * tok_count, width)
    slot_latent = jnp.einsum(
        "ts,td->sd", selected_half, current, preferred_element_type=jnp.float32
    )
    slot_latent = slot_latent.astype(jnp.bfloat16).reshape(
        ep_size, local_experts, image_count * capacity, width
    )
    slot_noise = jnp.einsum(
        "ts,td->sd", selected_half, noise_now, preferred_element_type=jnp.float32
    )
    image_factor = advantages * (drift_gain / noise_gain)
    slot_scale = slot_gate * image_factor[image_of_slot]
    home_cot = (
        (slot_scale[:, None] * slot_noise)
        .astype(jnp.bfloat16)
        .reshape(ep_size, local_experts, image_count * capacity, width)
    )
    returned, hidden = expert_pass(
        lax.all_to_all(slot_latent, "ep", split_axis=0, concat_axis=0, tiled=True), w_up, w_down
    )
    returned, hidden, cotangent = (
        returned,
        hidden,
        lax.all_to_all(home_cot, "ep", split_axis=0, concat_axis=0, tiled=True),
    )
    back_rows = returned.reshape(total_slots, width)
    taken = jnp.take(back_rows, slot_ids, axis=0)
    velocity = jnp.sum(flat_weights[..., None] * taken.astype(jnp.float32), axis=1)
    moved = (
        keep_gain * current.astype(jnp.float32)
        + drift_gain * velocity
        + noise_gain * noise_now.astype(jnp.float32)
    )
    current = moved.astype(jnp.bfloat16)
    kept_hidden = [hidden]
    kept_cot = [cotangent]
    rate = 10.0 / math.sqrt(tok_count * ep_size * top_count * image_count * group_size / experts)
    total = jnp.zeros((hidden_units, local_experts, width), jnp.float32)
    for hidden, cotangent in zip(kept_hidden, kept_cot):
        total = jnp.einsum("jlch,jlcd->hld", hidden, cotangent, preferred_element_type=jnp.float32)
    summed = lax.psum(
        (total * (1.0 / math.sqrt(hidden_units)))
        .reshape(hidden_units, local_experts * width)
        .astype(jnp.bfloat16),
        ("role", "dp"),
    ).astype(jnp.float32)
    summed = jnp.transpose(summed.reshape(hidden_units, local_experts, width), (1, 0, 2))
    new_down = (w_down.astype(jnp.float32) + rate * summed).astype(jnp.bfloat16)
    return (current.reshape(image_count, tok_count, width), new_down)


def solution(mesh):
    in_specs = (
        P(("role", "dp"), "ep", None),
        P(None, ("role", "dp"), "ep", None),
        P(None, ("role", "dp"), "ep", None),
        P(None, ("role", "dp"), "ep", None),
        P(("role", "dp")),
        P("ep", None, ("role", "dp"), None),
    )
    out_specs = (P(("role", "dp"), "ep", None), P("ep", None, None))
    return jax.shard_map(
        per_device, mesh=mesh, in_specs=in_specs, out_specs=out_specs, check_vma=False
    )
```

profile of v0, /device:TPU:1, one launch (start us, length us, event | category | flops | bytes accessed | tf_op | source)
XLA Modules:
  0.0 347.3 jit_solution(13016884792895209371)
XLA Ops:
  9.0 1.8 reduce-window.6
  11.6 0.8 mul.176
  13.5 1.9 convolution_convert_fusion
  15.4 2.5 reshape.262
  17.9 17.5 %all-to-all-start = ((bf16[64,1,14,1536]{3,2,1,0:T(8,128)(2,1)}), bf16[64,1,14,1536]{3,2,1,0:T(8,128)(2,1)}, u32[]{:S(2)}, u32[]{:S(2)}) async-start(bf16[64,1,14,1536]{3,2,1,0:T(8,128)(2,1)} %bitcast.3), calls=%async_computation | async-start | bytes 6291456 | tf_op jit(solution)/shard_map/all_to_all | solution.py:94
  36.8 1.3 fusion.30
  38.1 0.9 multiply_convert_fusion
  39.1 2.6 reshape.268
  41.6 70.5 %all-to-all-done = bf16[64,1,14,1536]{3,2,1,0:T(8,128)(2,1)} async-done(((bf16[64,1,14,1536]{3,2,1,0:T(8,128)(2,1)}), bf16[64,1,14,1536]{3,2,1,0:T(8,128)(2,1)}, u32[]{:S(2)}, u32[]{:S(2)}) %all-to-all-start) | async-done | bytes 2752544 | tf_op jit(solution)/shard_map/all_to_all | solution.py:94
  112.1 24.3 %all-to-all-start.2 = ((bf16[64,1,14,1536]{3,2,1,0:T(8,128)(2,1)}), bf16[64,1,14,1536]{3,2,1,0:T(8,128)(2,1)S(1)}, u32[]{:S(2)}, u32[]{:S(2)}) async-start(bf16[64,1,14,1536]{3,2,1,0:T(8,128)(2,1)} %bitcast.23), calls=%async_computation.2 | async-start | bytes 6291456 | tf_op jit(solution)/shard_map/all_to_all | solution.py:99
  136.5 8.1 %fusion.21 = bf16[64,14,768]{2,0,1:T(8,128)(2,1)S(1)} fusion(bf16[1,2,768,1536]{3,2,1,0:T(8,128)(2,1)} %all-gather.2.cloned.1.call-done, bf16[64,1,14,1536]{3,2,1,0:T(8,128)(2,1)} %all-to-all-done), kind=kOutput, calls=%fused_computation.31 | convolution fusion | flops 2120810496 | bytes 6881280 | tf_op jit(solution)/shard_map/jlcd,lhd->jlch/dot_general | solution.py:41
  144.5 2.3 fusion.1
  146.8 3.2 copy.71
  150.0 61.7 %all-to-all-done.2 = bf16[64,1,14,1536]{3,2,1,0:T(8,128)(2,1)S(1)} async-done(((bf16[64,1,14,1536]{3,2,1,0:T(8,128)(2,1)}), bf16[64,1,14,1536]{3,2,1,0:T(8,128)(2,1)S(1)}, u32[]{:S(2)}, u32[]{:S(2)}) %all-to-all-start.2) | async-done | bytes 2752544 | tf_op jit(solution)/shard_map/all_to_all | solution.py:99
  211.7 20.9 %all-to-all-start.1 = ((bf16[64,1,14,1536]{3,2,1,0:T(8,128)(2,1)}), bf16[64,1,14,1536]{3,2,1,0:T(8,128)(2,1)}, u32[]{:S(2)}, u32[]{:S(2)}) async-start(bf16[64,1,14,1536]{3,2,1,0:T(8,128)(2,1)} %copy.71), calls=%async_computation.1 | async-start | bytes 6291456 | tf_op jit(solution)/shard_map/all_to_all | solution.py:48
  232.9 7.0 %fusion.2 = bf16[768,1536]{1,0:T(8,128)(2,1)} fusion(bf16[64,14,768]{2,0,1:T(8,128)(2,1)} %copy-done.5, bf16[64,1,14,1536]{3,2,1,0:T(8,128)(2,1)S(1)} %all-to-all-done.2), kind=kOutput, calls=%fused_computation.10 | convolution fusion | flops 2116288512 | bytes 6488064 | tf_op jit(solution)/shard_map/jlch,jlcd->hld/dot_general | solution.py:115
  241.9 0.8 copy.68
  242.7 77.1 %all-reduce.2.cloned.1.call-done = bf16[768,1536]{1,0:T(8,128)(2,1)} async-done(((bf16[768,1536]{1,0:T(8,128)(2,1)}), bf16[768,1536]{1,0:T(8,128)(2,1)}) %all-reduce.2.cloned.1.call-update) | async-done | bytes 2359312 | tf_op jit(solution)/shard_map/psum | solution.py:116
  319.8 4.5 %fusion.16 = bf16[1,768,1536]{2,1,0:T(8,128)(2,1)} fusion(bf16[768,1536]{1,0:T(8,128)(2,1)} %all-reduce.2.cloned.1.call-done, bf16[1,2,768,1536]{3,2,1,0:T(8,128)(2,1)} %all-gather.2.cloned.1.call-done), kind=kLoop, calls=%fused_computation.27 | loop fusion | flops 5898240 | bytes 7077888 | tf_op jit(solution)/shard_map/convert_element_type | solution.py:123
  324.3 3.8 %reshape.267 = bf16[896,1536]{1,0:T(8,128)(2,1)S(1)} reshape(bf16[64,1,14,1536]{3,2,1,0:T(8,128)(2,1)} %all-to-all-done.1) | data formatting | bytes 5505024 | tf_op jit(solution)/shard_map/reshape | solution.py:101
  328.1 3.8 %gather_fusion = bf16[768,1536]{1,0:T(8,128)(2,1)} fusion(bf16[896,1536]{1,0:T(8,128)(2,1)S(1)} %reshape.267, s32[1024]{0:T(1024)S(1)} %pad_clamp_fusion), kind=kCustom, calls=%fused_computation | custom fusion | bytes 4721664 | tf_op jit(solution)/shard_map/jit(_take)/gather | solution.py:102
  331.9 3.5 %reshape.271 = bf16[128,6,1536]{2,1,0:T(8,128)(2,1)S(1)} reshape(bf16[768,1536]{1,0:T(8,128)(2,1)} %gather_fusion) | data formatting | bytes 4718592 | tf_op jit(solution)/shard_map/jit(_take)/gather | solution.py:102
  335.4 4.0 %multiply_reduce_fusion = f32[128,1536]{1,0:T(8,128)S(1)} fusion(bf16[128,6,1536]{2,1,0:T(8,128)(2,1)S(1)} %reshape.271, f32[128,6]{1,0:T(8,128)} %copy.61, pred[128,6]{1,0:T(8,128)(4,1)S(1)} %copy.68), kind=kLoop, calls=%fused_computation.1 | loop fusion | flops 4521984 | bytes 3149568 | tf_op jit(solution)/shard_map/reduce_sum | solution.py:103
  339.5 0.9 fusion.24
  (48 shorter events, 7.4 us)
Async XLA Ops:
  11.6 6.4 %copy-start.3 = (s32[128]{0:T(128)}, s32[128]{0:T(128)S(1)}, u32[]{:S(2)}) copy-start(s32[128]{0:T(128)S(1)} %add.131) | copy-start | bytes 1540
  17.9 18.3 %copy-start.4 = (f32[2]{0:T(128)S(1)}, f32[2]{0:T(128)}, u32[]{:S(2)}) copy-start(f32[2]{0:T(128)} %param.10) | copy-start | bytes 28
  17.9 20.2 %copy-start = (bf16[1,2,64,1536]{3,2,1,0:T(8,128)(2,1)S(1)}, bf16[1,2,64,1536]{3,2,1,0:T(8,128)(2,1)}, u32[]{:S(2)}) copy-start(bf16[1,2,64,1536]{3,2,1,0:T(8,128)(2,1)} %param.7) | copy-start | bytes 1179652
  17.9 94.2 %all-to-all-start = ((bf16[64,1,14,1536]{3,2,1,0:T(8,128)(2,1)}), bf16[64,1,14,1536]{3,2,1,0:T(8,128)(2,1)}, u32[]{:S(2)}, u32[]{:S(2)}) async-start(bf16[64,1,14,1536]{3,2,1,0:T(8,128)(2,1)} %bitcast.3), calls=%async_computation | async-start | bytes 6291456 | tf_op jit(solution)/shard_map/all_to_all | solution.py:94
  35.4 101.0 %all-gather.2.cloned.1.call-start = ((), (), s32[]{:S(2)}) async-start(), calls=%async_computation.3 | async-start | bytes 5308416 | tf_op jit(solution)/shard_map/all_gather | solution.py:65
  112.1 99.6 %all-to-all-start.2 = ((bf16[64,1,14,1536]{3,2,1,0:T(8,128)(2,1)}), bf16[64,1,14,1536]{3,2,1,0:T(8,128)(2,1)S(1)}, u32[]{:S(2)}, u32[]{:S(2)}) async-start(bf16[64,1,14,1536]{3,2,1,0:T(8,128)(2,1)} %bitcast.23), calls=%async_computation.2 | async-start | bytes 6291456 | tf_op jit(solution)/shard_map/all_to_all | solution.py:99
  136.4 8.1 %copy-start.2 = (bf16[1,2,768,1536]{3,2,1,0:T(8,128)(2,1)S(1)}, bf16[1,2,768,1536]{3,2,1,0:T(8,128)(2,1)}, u32[]{:S(2)}) copy-start(bf16[1,2,768,1536]{3,2,1,0:T(8,128)(2,1)} %all-gather.2.cloned.1.call-done) | copy-start | bytes 14155780
  144.5 2.3 copy-start.5
  211.7 112.6 %all-to-all-start.1 = ((bf16[64,1,14,1536]{3,2,1,0:T(8,128)(2,1)}), bf16[64,1,14,1536]{3,2,1,0:T(8,128)(2,1)}, u32[]{:S(2)}, u32[]{:S(2)}) async-start(bf16[64,1,14,1536]{3,2,1,0:T(8,128)(2,1)} %copy.71), calls=%async_computation.1 | async-start | bytes 6291456 | tf_op jit(solution)/shard_map/all_to_all | solution.py:48
  232.6 87.2 %all-reduce.2.cloned.1.call-start = ((), (), s32[]{:S(2)}) async-start(), calls=%async_computation.4 | async-start | bytes 4718592 | tf_op jit(solution)/shard_map/psum | solution.py:116
  335.4 4.1 %copy-start.1 = (bf16[2,64,1536]{2,1,0:T(8,128)(2,1)S(1)}, bf16[2,64,1536]{2,1,0:T(8,128)(2,1)}, u32[]{:S(2)}) copy-start(bf16[2,64,1536]{2,1,0:T(8,128)(2,1)} %param.6) | copy-start | bytes 1179652
Sparse Core Ops, SparseCore 0:
  38.4 41.0 all-gather.1
  240.1 79.6 all-reduce.1
where the time goes:
time: 349 us; the launch traced here: 347 us
  waiting for transfers between devices  210 us (60%)
  starting transfers between devices  63 us (18%)
  local copies, waits for them, and re-layouts  24.5 us (7%)
  matrix products  20.2 us (6%)
  other arithmetic  15.4 us (4%)
  between operations  14.3 us (4%)
    psum x1, waiting for transfers between devices, per_device(): lax.psum((total * (1.0 / math.sqrt(hidden_units))).reshape(hidden_units,...  77.1 us
    all_to_all x1, waiting for transfers between devices, per_device(): lax.all_to_all(slot_latent, 'ep', split_axis=0, concat_axis=0, tiled=True)  70.5 us
    all_to_all x1, waiting for transfers between devices, per_device(): lax.all_to_all(home_cot, 'ep', split_axis=0, concat_axis=0, tiled=True)  61.7 us
    all_to_all x1, starting transfers between devices, per_device(): lax.all_to_all(home_cot, 'ep', split_axis=0, concat_axis=0, tiled=True)  24.3 us
    all_to_all x1, starting transfers between devices, expert_pass(): lax.all_to_all(output.astype(jnp.bfloat16), 'ep', split_axis=0, concat_ax...  20.9 us
    all_to_all x1, starting transfers between devices, per_device(): lax.all_to_all(slot_latent, 'ep', split_axis=0, concat_axis=0, tiled=True)  17.5 us
    dot_general x1, matrix products, expert_pass(): jnp.einsum('jlcd,lhd->jlch', inputs, w_up, preferred_element_type=jnp.flo...  8.06 us
    gather x2, local copies, waits for them, and re-layouts, per_device(): taken = jnp.take(back_rows, slot_ids, axis=0)  7.35 us
  transfers between devices with their start and end apart: 5, of which 3 were waited for; matrix products, arithmetic and copies ran while one was open for 10% of the time, Pallas kernels for 0%

commit v1 on v0

v1 whole, which is shorter than its diff:
```python
import functools
import math

import jax
import jax.numpy as jnp
from jax import lax
from jax.experimental import pallas as pl
from jax.experimental.pallas import tpu as pltpu
from jax.sharding import PartitionSpec as P

CAP = 7
SIDE = 8
MESH = pl.DeviceIdType.MESH
F32 = jnp.float32
BF16 = jnp.bfloat16


def coefficients(section):
    moment = 0.95 - 0.4 * section
    noise_level = 0.3 * math.sqrt(moment / (1.0 - moment))
    factor = noise_level * noise_level / (2.0 * moment)
    keep_gain = 1.0 - 0.4 * factor
    drift_gain = -0.4 * (1.0 + factor * (1.0 - moment))
    noise_gain = noise_level * math.sqrt(0.4)
    return (keep_gain, drift_gain, noise_gain)


def mm(a, b):
    return jnp.dot(a, b, preferred_element_type=F32)


def iota(shape, dim):
    return lax.broadcasted_iota(jnp.int32, shape, dim)


def kernel(
    sizes,
    ids_ref,
    gate_ref,
    adv_ref,
    lat_ref,
    noise_ref,
    shard_ref,
    fin_ref,
    nd_ref,
    meta_s,
    meta_r,
    gath,
    sel,
    selg,
    selgt,
    scale,
    send_a,
    send_b,
    recv_l,
    recv_n,
    recv_o,
    wbuf,
    perm,
    hid,
    hidp,
    term,
    gx,
    gsend,
    grecv,
    red_r,
    meta_sem,
    gath_sem,
    l_sem,
    n_sem,
    o_sem,
    red_sem,
    wx_sem,
    wc_sem,
    gc_sem,
    gr_sem,
    dx_sem,
    dc_sem,
):
    images, n_role, n_dp, rate = sizes
    toks = lat_ref.shape[0]
    per_image = toks // images
    width = lat_ref.shape[1]
    half = width // 2
    hidden_units = wbuf.shape[1]
    rows = shard_ref.shape[1]
    slots = images * CAP
    blk = SIDE * slots
    total = SIDE * blk
    keep_gain, drift_gain, noise_gain = coefficients(0)

    role = lax.axis_index("role")
    ep = lax.axis_index("ep")
    dp = lax.axis_index("dp")
    z, y = lax.div(ep, SIDE), lax.rem(ep, SIDE)
    other = 1 - dp
    d1 = 1 - 2 * dp
    mine = role * n_dp + dp

    def pos_g(ax):
        return z * (1 - ax) + y * ax

    def pos_x(ax):
        return y * (1 - ax) + z * ax

    def dev_g(ax, i):
        return {"ep": (i * SIDE + y) * (1 - ax) + (z * SIDE + i) * ax}

    def dev_x(ax, i):
        return {"ep": (z * SIDE + i) * (1 - ax) + (i * SIDE + y) * ax}

    def ring(i):
        return lax.rem(i + 2 * SIDE, SIDE)

    def role_at(i):
        return lax.rem(role + n_role + i, n_role)

    def copy(src, dst, sems, at, dev):
        return pltpu.make_async_remote_copy(
            src_ref=src,
            dst_ref=dst,
            send_sem=sems.at[(0,) + at],
            recv_sem=sems.at[(1,) + at],
            device_id=dev,
            device_id_type=MESH,
        )

    def each(low, high, body):
        def step(i, carry):
            body(i)
            return carry

        lax.fori_loop(low, high, step, 0)

    def wrows(q):
        return pl.ds(pl.multiple_of(q * rows, rows), rows)

    def brows(i):
        return pl.ds(pl.multiple_of(i * blk, blk), blk)

    def trows(i):
        return pl.ds(pl.multiple_of(i * toks, toks), toks)

    barrier = pltpu.get_barrier_semaphore()

    def greet(j):
        for ax in (0, 1):
            pl.semaphore_signal(
                barrier, inc=1, device_id=dev_x(ax, ring(pos_x(ax) + j)), device_id_type=MESH
            )

    each(1, SIDE, greet)
    for i in range(1, n_role):
        pl.semaphore_signal(barrier, inc=1, device_id={"role": role_at(i)}, device_id_type=MESH)
    pl.semaphore_signal(barrier, inc=1, device_id={"dp": other}, device_id_type=MESH)

    lane = iota((toks, toks), 1)
    row = iota((toks, toks), 0)
    same = jnp.where(lane >= per_image, 1, 0) == jnp.where(row >= per_image, 1, 0)
    before = jnp.where(same & (row < lane), 1.0, 0.0).astype(BF16)
    first_slot = jnp.where(lane >= per_image, float(CAP), 0.0)
    ids = ids_ref[...]
    gates = gate_ref[...]
    for ax in (0, 1):
        named = ids if ax == 0 else (ids & (SIDE - 1)) * SIDE + (ids >> 3)
        hit = jnp.zeros((toks, toks), F32)
        gate = jnp.zeros((toks, toks), F32)
        for k in range(ids.shape[1]):
            at = named[:, k : k + 1] == lane
            hit = jnp.where(at, 1.0, hit)
            gate = jnp.where(at, gates[:, k : k + 1], gate)
        hit_t = hit.T
        gate_t = gate.T
        rank = mm(hit_t.astype(BF16), before) + first_slot
        place = jnp.where(hit_t > 0.5, rank, -1000.0)
        for i in range(SIDE):
            meta_s[ax, i, 0:SIDE, :] = place[i * SIDE : (i + 1) * SIDE]
            meta_s[ax, i, SIDE : 2 * SIDE, :] = gate_t[i * SIDE : (i + 1) * SIDE]
        cols = slice(ax * half, (ax + 1) * half)
        gath[0, ax, pos_g(ax)] = lat_ref[:, cols]
        gath[1, ax, pos_g(ax)] = noise_ref[:, cols]
        meta_r[ax, pos_g(ax)] = meta_s[ax, pos_g(ax)]
    wbuf[:, wrows(mine), :] = shard_ref[...]

    pl.semaphore_wait(barrier, 2 * (SIDE - 1) + n_role)

    def gath_hop(kind, ax, way, hop):
        step = d1 * (1 - 2 * way)
        slot = ring(pos_g(ax) - step * (hop - 1))
        block = gath.at[kind, ax, slot]
        return copy(block, block, gath_sem, (kind, ax, way, hop - 1), dev_g(ax, ring(pos_g(ax) + step)))

    def gath_wait(kind, ax, way, hop):
        step = d1 * (1 - 2 * way)
        block = gath.at[kind, ax, ring(pos_g(ax) - step * hop)]
        copy(block, block, gath_sem, (kind, ax, way, hop - 1), dev_g(ax, ring(pos_g(ax) + step))).wait_recv()

    def meta_copy(ax, j):
        return copy(
            meta_s.at[ax, ring(pos_g(ax) + j)],
            meta_r.at[ax, pos_g(ax)],
            meta_sem,
            (ax, j - 1),
            dev_g(ax, ring(pos_g(ax) + j)),
        )

    def meta_start(j):
        for ax in (0, 1):
            meta_copy(ax, j).start()

    each(1, SIDE, meta_start)
    for kind in (0, 1):
        for ax in (0, 1):
            for way in (0, 1):
                gath_hop(kind, ax, way, 1).start()

    def w_role(i):
        return copy(shard_ref, wbuf.at[:, wrows(mine), :], wx_sem, (i - 1,), {"role": role_at(i)})

    def w_core(i):
        q = role_at(-i) * n_dp + dp
        block = wbuf.at[:, wrows(q), :]
        return copy(block, block, wc_sem, (i,), {"dp": other})

    for i in range(1, n_role):
        w_role(i).start()
    w_core(0).start()

    def forward(hop):
        for kind in (0, 1):
            for ax in (0, 1):
                for way in (0, 1):
                    if hop <= 4 - way:
                        gath_wait(kind, ax, way, hop)
                        if hop + 1 <= 4 - way:
                            gath_hop(kind, ax, way, hop + 1).start()

    def meta_wait(j):
        for ax in (0, 1):
            slot = meta_r.at[ax, ring(pos_g(ax) - j)]
            copy(slot, slot, meta_sem, (ax, j - 1), dev_g(ax, ring(pos_g(ax) + j))).wait_recv()

    each(1, SIDE, meta_wait)
    gain = drift_gain / noise_gain
    lane1 = iota((1, toks), 1)
    factor = jnp.where(lane1 >= per_image, adv_ref[1] * gain, adv_ref[0] * gain)
    slot_row = iota((blk, toks), 0).astype(F32)

    def build(ax):
        def one(e):
            scaled = jnp.zeros((blk, 1), F32)
            for s in range(SIDE):
                place = meta_r[ax, s, pl.ds(e, 1), :]
                gate = meta_r[ax, s, pl.ds(SIDE + e, 1), :]
                at = (slot_row - float(slots * s)) == place
                cols = slice(s * toks, (s + 1) * toks)
                sel[ax, e, :, cols] = jnp.where(at, 1.0, 0.0).astype(BF16)
                selg[brows(e), cols] = jnp.where(at, gate, 0.0).astype(BF16)
                scaled = scaled + jnp.sum(jnp.where(at, gate * factor, 0.0), axis=1, keepdims=True)
            scale[ax, e] = jnp.broadcast_to(scaled, (blk, toks))

        each(0, SIDE, one)

        def turn(s):
            cols = pl.ds(pl.multiple_of(s * toks, toks), toks)
            for b in range(total // toks):
                part = selg[b * toks : (b + 1) * toks, cols].astype(F32)
                selgt[ax, s, :, b * toks : (b + 1) * toks] = part.T.astype(BF16)

        each(0, SIDE, turn)

    build(0)
    forward(1)
    build(1)
    forward(2)
    r_iota = iota((total, 1), 0)
    outer = lax.div(r_iota, blk)
    inner = lax.div(r_iota - outer * blk, slots)
    target = inner * blk + outer * slots + (r_iota - outer * blk - inner * slots)
    perm[...] = jnp.where(iota((total, total), 1) == target, 1.0, 0.0).astype(BF16)
    forward(3)
    for i in range(1, n_role):
        q = role_at(-i) * n_dp + dp
        block = wbuf.at[:, wrows(q), :]
        copy(block, block, wx_sem, (i - 1,), {"role": role_at(i)}).wait_recv()
        w_core(i).start()
    forward(4)

    def x_copy(buf, dst, sems, ax, j):
        to = ring(pos_x(ax) + j)
        return copy(buf.at[ax, brows(to), :], dst.at[ax, brows(pos_x(ax)), :], sems, (ax, j - 1), dev_x(ax, to))

    def x_wait(dst, sems):
        def one(j):
            for ax in (0, 1):
                block = dst.at[ax, brows(ring(pos_x(ax) - j)), :]
                copy(block, block, sems, (ax, j - 1), dev_x(ax, ring(pos_x(ax) + j))).wait_recv()

        each(1, SIDE, one)

    def x_sent(buf, dst, sems):
        def one(j):
            for ax in (0, 1):
                x_copy(buf, dst, sems, ax, j).wait_send()

        each(1, SIDE, one)

    def picked(kind, ax, e):
        rows_ = gath[kind, ax].reshape(SIDE * toks, half)
        return mm(sel[ax, e], rows_)

    def pack_l(j):
        def one(ax):
            to = ring(pos_x(ax) + j)
            send_a[ax, brows(to), :] = picked(0, ax, to).astype(BF16)
            x_copy(send_a, recv_l, l_sem, ax, j).start()

        each(0, 2, one)

    each(1, SIDE, pack_l)

    def own_l(ax):
        here = pos_x(ax)
        recv_l[ax, brows(here), :] = picked(0, ax, here).astype(BF16)

    each(0, 2, own_l)

    def pack_n(j):
        def one(ax):
            to = ring(pos_x(ax) + j)
            col = scale[ax, to][:, 0:1]
            send_b[ax, brows(to), :] = (col * picked(1, ax, to)).astype(BF16)

        each(0, 2, one)

    each(0, SIDE, pack_n)
    for ax in (0, 1):
        recv_n[ax, brows(pos_x(ax)), :] = send_b[ax, brows(pos_x(ax)), :]
    x_wait(recv_l, l_sem)

    def start_n(j):
        for ax in (0, 1):
            x_copy(send_b, recv_n, n_sem, ax, j).start()

    each(1, SIDE, start_n)

    for i in range(n_role):
        q = role_at(-i) * n_dp + other
        block = wbuf.at[:, wrows(q), :]
        copy(block, block, wc_sem, (i,), {"dp": other}).wait_recv()
    x_sent(send_a, recv_l, l_sem)
    chunk = 256

    def cols_at(n):
        return pl.ds(pl.multiple_of(n * chunk, chunk), chunk)

    def align(n):
        send_a[1, :, cols_at(n)] = mm(perm[...], recv_l[1, :, cols_at(n)]).astype(BF16)

    each(0, half // chunk, align)

    def up(n):
        def nt(a, b):
            return lax.dot_general(a, b, (((1,), (1,)), ((), ())), preferred_element_type=F32)

        hrows = pl.ds(pl.multiple_of(n * chunk, chunk), chunk)
        pre = nt(recv_l[0], wbuf[0, hrows, 0:half]) + nt(send_a[1], wbuf[0, hrows, half:width])
        hidden = jax.nn.gelu(pre * (1.0 / math.sqrt(width)), approximate=True).astype(BF16)
        hid[:, cols_at(n)] = hidden
        hidp[:, cols_at(n)] = mm(perm[...], hidden).astype(BF16)

    each(0, hidden_units // chunk, up)
    down_gain = 1.0 / math.sqrt(hidden_units)

    for ax in (0, 1):
        source = hid if ax == 0 else hidp

        def down(n, ax=ax, source=source):
            cols = pl.ds(pl.multiple_of(ax * half + n * chunk, chunk), chunk)
            send_a[ax, :, cols_at(n)] = (mm(source[...], wbuf[1, :, cols]) * down_gain).astype(BF16)

        each(0, half // chunk, down)

        def start_o(j, ax=ax):
            x_copy(send_a, recv_o, o_sem, ax, j).start()

        each(1, SIDE, start_o)
        recv_o[ax, brows(pos_x(ax)), :] = send_a[ax, brows(pos_x(ax)), :]

    x_wait(recv_n, n_sem)
    for ax in (0, 1):
        source = hid if ax == 0 else hidp

        def outer_product(m, ax=ax, source=source):
            part = lax.dot_general(
                source[:, cols_at(m)], recv_n[ax], (((0,), (0,)), ((), ())), preferred_element_type=F32
            )
            mrows = pl.ds(pl.multiple_of(m * chunk, chunk), chunk)
            term[mrows, ax * half : (ax + 1) * half] = (part * down_gain).astype(BF16)

        each(0, hidden_units // chunk, outer_product)

    def g_core(i):
        return copy(term.at[wrows(i * n_dp + other), :], gx.at[i], gc_sem, (i,), {"dp": other})

    for i in range(n_role):
        g_core(i).start()
    x_sent(send_b, recv_n, n_sem)

    def weighed(ax, to):
        return mm(selgt[ax, to], recv_o[ax])

    def red_slot(way, k):
        return way * 4 + k - 1

    def red_copy(ax, way, k):
        step = d1 * (1 - 2 * way)
        slot = red_slot(way, k)
        return copy(
            send_b.at[ax, trows(slot), :],
            red_r.at[ax, trows(slot), :],
            red_sem,
            (ax, slot),
            dev_g(ax, ring(pos_g(ax) + step)),
        )

    def red_arrived(ax, way, k):
        slot = red_slot(way, k)
        block = red_r.at[ax, trows(slot), :]
        copy(block, block, red_sem, (ax, slot), dev_g(ax, ring(pos_g(ax) + d1 * (1 - 2 * way)))).wait_recv()
        return red_r[ax, trows(slot), :].astype(F32)

    def reduce_step(k):
        def one(ax):
            for way in (0, 1):
                hops = 4 - way
                if k > hops:
                    continue
                step = d1 * (1 - 2 * way)
                value = weighed(ax, ring(pos_g(ax) + step * (hops + 1 - k)))
                if k > 1:
                    value = value + red_arrived(ax, way, k - 1)
                send_b[ax, trows(red_slot(way, k)), :] = value.astype(BF16)
                red_copy(ax, way, k).start()

        each(0, 2, one)

    x_wait(recv_o, o_sem)
    reduce_step(1)

    def g_role(i):
        return copy(gsend.at[i - 1], grecv.at[i - 1], gr_sem, (i - 1,), {"role": role_at(i)})

    for i in range(n_role):
        copy(gx.at[i], gx.at[i], gc_sem, (i,), {"dp": other}).wait_recv()
    for i in range(1, n_role):
        to = role_at(i)
        gsend[i - 1] = (term[wrows(to * n_dp + dp), :].astype(F32) + gx[to].astype(F32)).astype(BF16)
        g_role(i).start()

    reduce_step(2)
    reduce_step(3)

    for i in range(1, n_role):
        copy(grecv.at[i - 1], grecv.at[i - 1], gr_sem, (i - 1,), {"role": role_at(i)}).wait_recv()
    grad = term[wrows(mine), :].astype(F32) + gx[role].astype(F32)
    for i in range(1, n_role):
        grad = grad + grecv[i - 1].astype(F32)
    nd_ref[wrows(mine), :] = (wbuf[1, wrows(mine), :].astype(F32) + rate * grad).astype(BF16)

    def d_role(i):
        block = nd_ref.at[wrows(mine), :]
        return copy(block, block, dx_sem, (i - 1,), {"role": role_at(i)})

    def d_core(i):
        block = nd_ref.at[wrows(role_at(-i) * n_dp + dp), :]
        return copy(block, block, dc_sem, (i,), {"dp": other})

    for i in range(1, n_role):
        d_role(i).start()
    d_core(0).start()

    reduce_step(4)

    for i in range(1, n_role):
        block = nd_ref.at[wrows(role_at(-i) * n_dp + dp), :]
        copy(block, block, dx_sem, (i - 1,), {"role": role_at(i)}).wait_recv()
        d_core(i).start()

    for ax in (0, 1):
        cols = slice(ax * half, (ax + 1) * half)
        velocity = weighed(ax, pos_g(ax)) + red_arrived(ax, 1, 3) + red_arrived(ax, 0, 4)
        moved = (
            keep_gain * lat_ref[:, cols].astype(F32)
            + drift_gain * velocity
            + noise_gain * noise_ref[:, cols].astype(F32)
        )
        fin_ref[:, cols] = moved.astype(BF16)

    for i in range(n_role):
        block = nd_ref.at[wrows(role_at(-i) * n_dp + other), :]
        copy(block, block, dc_sem, (i,), {"dp": other}).wait_recv()

    def meta_sent(j):
        for ax in (0, 1):
            meta_copy(ax, j).wait_send()

    each(1, SIDE, meta_sent)
    for kind in (0, 1):
        for ax in (0, 1):
            for way in (0, 1):
                for hop in range(1, 5 - way):
                    gath_hop(kind, ax, way, hop).wait_send()
    x_sent(send_a, recv_o, o_sem)
    for ax in (0, 1):
        for way in (0, 1):
            for k in range(1, 5 - way):
                red_copy(ax, way, k).wait_send()
    for i in range(1, n_role):
        w_role(i).wait_send()
        g_role(i).wait_send()
        d_role(i).wait_send()
    for i in range(n_role):
        w_core(i).wait_send()
        g_core(i).wait_send()
        d_core(i).wait_send()


def per_device(latents, noise, expert_ids, gate_values, advantages, expert_pair):
    n_role, n_dp, n_ep = lax.axis_size("role"), lax.axis_size("dp"), lax.axis_size("ep")
    images, tok_count, width = latents.shape
    top = expert_ids.shape[3]
    toks = images * tok_count
    rows = expert_pair.shape[2]
    hidden_units = rows * n_role * n_dp
    experts = expert_pair.shape[0] * n_ep
    half = width // 2
    slots = images * CAP
    blk = SIDE * slots
    total = SIDE * blk
    rate = 10.0 / math.sqrt(tok_count * n_ep * top * images * n_role * n_dp / experts)
    vmem = pl.BlockSpec(memory_space=pltpu.VMEM)
    dma = pltpu.SemaphoreType.DMA
    fin, new_down = pl.pallas_call(
        functools.partial(kernel, (images, n_role, n_dp, rate)),
        out_shape=(
            jax.ShapeDtypeStruct((toks, width), BF16),
            jax.ShapeDtypeStruct((hidden_units, width), BF16),
        ),
        in_specs=[vmem, vmem, pl.BlockSpec(memory_space=pltpu.SMEM), vmem, vmem, vmem],
        out_specs=(vmem, vmem),
        scratch_shapes=[
            pltpu.VMEM((2, SIDE, 2 * SIDE, toks), F32),
            pltpu.VMEM((2, SIDE, 2 * SIDE, toks), F32),
            pltpu.VMEM((2, 2, SIDE, toks, half), BF16),
            pltpu.VMEM((2, SIDE, blk, SIDE * toks), BF16),
            pltpu.VMEM((total, SIDE * toks), BF16),
            pltpu.VMEM((2, SIDE, toks, total), BF16),
            pltpu.VMEM((2, SIDE, blk, toks), F32),
            pltpu.VMEM((2, total, half), BF16),
            pltpu.VMEM((2, total, half), BF16),
            pltpu.VMEM((2, total, half), BF16),
            pltpu.VMEM((2, total, half), BF16),
            pltpu.VMEM((2, total, half), BF16),
            pltpu.VMEM((2, hidden_units, width), BF16),
            pltpu.VMEM((total, total), BF16),
            pltpu.VMEM((total, hidden_units), BF16),
            pltpu.VMEM((total, hidden_units), BF16),
            pltpu.VMEM((hidden_units, width), BF16),
            pltpu.VMEM((n_role, rows, width), BF16),
            pltpu.VMEM((n_role - 1, rows, width), BF16),
            pltpu.VMEM((n_role - 1, rows, width), BF16),
            pltpu.VMEM((2, 7 * toks, half), BF16),
            dma((2, 2, SIDE - 1)),
            dma((2, 2, 2, 2, 4)),
            dma((2, 2, SIDE - 1)),
            dma((2, 2, SIDE - 1)),
            dma((2, 2, SIDE - 1)),
            dma((2, 2, 7)),
            dma((2, n_role - 1)),
            dma((2, n_role)),
            dma((2, n_role)),
            dma((2, n_role - 1)),
            dma((2, n_role - 1)),
            dma((2, n_role)),
        ],
        compiler_params=pltpu.CompilerParams(
            collective_id=0, has_side_effects=True, vmem_limit_bytes=60 * 1024 * 1024
        ),
    )(
        expert_ids.reshape(toks, top),
        gate_values.reshape(toks, top),
        advantages,
        latents.reshape(toks, width),
        noise.reshape(toks, width),
        expert_pair.reshape(2, rows, width),
    )
    return (fin.reshape(images, tok_count, width), new_down.reshape(1, hidden_units, width))


def solution(mesh):
    in_specs = (
        P(("role", "dp"), "ep", None),
        P(None, ("role", "dp"), "ep", None),
        P(None, ("role", "dp"), "ep", None),
        P(None, ("role", "dp"), "ep", None),
        P(("role", "dp")),
        P("ep", None, ("role", "dp"), None),
    )
    out_specs = (P(("role", "dp"), "ep", None), P("ep", None, None))
    return jax.shard_map(
        per_device, mesh=mesh, in_specs=in_specs, out_specs=out_specs, check_vma=False
    )
```

time: 349 us -> 191 us (0.55)
  waiting for transfers between devices: 210 us -> 0 us
  Pallas kernels: 0 us -> 183 us
  starting transfers between devices: 63 us -> 0 us
  matrix products: 20.2 us -> 0 us
  local copies, waits for them, and re-layouts: 24.5 us -> 7.84 us
  other arithmetic: 15.4 us -> 0 us
  between operations: 14.3 us -> 0.64 us
    pallas_call x0 -> x1, Pallas kernels: none -> 183 us  [per_device(): pl.pallas_call(functools.partial(kernel, (images, n_role, n_dp, rate)), o...]
    all_to_all x3 -> x0, waiting for transfers between devices: 132 us -> none  [the longest x1 70.5 us: per_device(): lax.all_to_all(slot_latent, 'ep', split_axis=0, concat_axis=0, tiled=True)]
    psum x1 -> x0, waiting for transfers between devices: 77.1 us -> none  [per_device(): lax.psum((total * (1.0 / math.sqrt(hidden_units))).reshape(hidden_units,...]
    all_to_all x3 -> x0, starting transfers between devices: 62.7 us -> none  [the longest x1 24.3 us: per_device(): lax.all_to_all(home_cot, 'ep', split_axis=0, concat_axis=0, tiled=True)]
    dot_general x5 -> x0, matrix products: 20.2 us -> none  [the longest x1 8.06 us: expert_pass(): jnp.einsum('jlcd,lhd->jlch', inputs, w_up, preferred_element_type=jnp.flo...]
    reshape x3 -> x0, local copies, waits for them, and re-layouts: 8.86 us -> none  [the longest x1 3.78 us: per_device(): back_rows = returned.reshape(total_slots, width)]
    gather x3 -> x0, local copies, waits for them, and re-layouts: 7.93 us -> none  [the longest x2 7.35 us: per_device(): taken = jnp.take(back_rows, slot_ids, axis=0)]
    unnamed x13 -> x4, local copies, waits for them, and re-layouts: 0.81 us -> 7.84 us
  transfers between devices with their start and end apart: 5 -> 0, of which waited for: 3 -> 0; matrix products, arithmetic and copies ran while one was open for 10% -> 0% of each run, Pallas kernels for 0% -> 0%
where the time goes in v1:
time: 191 us
  Pallas kernels  183 us (96%)
  local copies, waits for them, and re-layouts  7.84 us (4%)
    pallas_call x1, Pallas kernels, per_device(): pl.pallas_call(functools.partial(kernel, (images, n_role, n_dp, rate)), o...  183 us
    unnamed x4, local copies, waits for them, and re-layouts  7.84 us

profile of v1, /device:TPU:1, one launch (start us, length us, event | category | flops | bytes accessed | tf_op | source)
XLA Modules:
  0.0 191.1 jit_solution(8405306837823010762)
XLA Ops:
  0.6 1.4 copy.8
  2.1 1.4 copy.9
  3.5 182.6 %shard_map.77 = (bf16[128,1536]{1,0:T(8,128)(2,1)}, bf16[768,1536]{1,0:T(8,128)(2,1)}) custom-call(s32[128,6]{1,0:T(8,128)} %bitcast.12, f32[128,6]{1,0:T(8,128)} %bitcast.13, f32[2]{0:T(128)} %adv_ref.1, bf16[128,1536]{1,0:T(8,128)(2,1)} %bitcast.10, bf16[128,1536]{1,0:T(8,128)(2,1)} %bitcast.11, bf16[2,96,1536]{2,1,0:T(8,128)(2,1)} %bitcast.8), custom_call_target="tpu_custom_call" | custom-call | tf_op jit(solution)/shard_map/pallas_call | solution.py:544
  186.1 1.8 copy.12
  187.9 3.2 %copy.13 = bf16[1,768,1536]{2,1,0:T(8,128)(2,1)} copy(bf16[1,768,1536]{2,1,0:T(8,128)(2,1)} %bitcast.7) | data formatting | bytes 4718592

commit v2 on v1

--- a/solution.py
+++ b/solution.py
@@ -64,6 +64,7 @@
     gsend,
     grecv,
     red_r,
+    vel,
     meta_sem,
     gath_sem,
     l_sem,
@@ -154,33 +155,10 @@
         pl.semaphore_signal(barrier, inc=1, device_id={"role": role_at(i)}, device_id_type=MESH)
     pl.semaphore_signal(barrier, inc=1, device_id={"dp": other}, device_id_type=MESH)
 
-    lane = iota((toks, toks), 1)
-    row = iota((toks, toks), 0)
-    same = jnp.where(lane >= per_image, 1, 0) == jnp.where(row >= per_image, 1, 0)
-    before = jnp.where(same & (row < lane), 1.0, 0.0).astype(BF16)
-    first_slot = jnp.where(lane >= per_image, float(CAP), 0.0)
-    ids = ids_ref[...]
-    gates = gate_ref[...]
     for ax in (0, 1):
-        named = ids if ax == 0 else (ids & (SIDE - 1)) * SIDE + (ids >> 3)
-        hit = jnp.zeros((toks, toks), F32)
-        gate = jnp.zeros((toks, toks), F32)
-        for k in range(ids.shape[1]):
-            at = named[:, k : k + 1] == lane
-            hit = jnp.where(at, 1.0, hit)
-            gate = jnp.where(at, gates[:, k : k + 1], gate)
-        hit_t = hit.T
-        gate_t = gate.T
-        rank = mm(hit_t.astype(BF16), before) + first_slot
-        place = jnp.where(hit_t > 0.5, rank, -1000.0)
-        for i in range(SIDE):
-            meta_s[ax, i, 0:SIDE, :] = place[i * SIDE : (i + 1) * SIDE]
-            meta_s[ax, i, SIDE : 2 * SIDE, :] = gate_t[i * SIDE : (i + 1) * SIDE]
         cols = slice(ax * half, (ax + 1) * half)
         gath[0, ax, pos_g(ax)] = lat_ref[:, cols]
         gath[1, ax, pos_g(ax)] = noise_ref[:, cols]
-        meta_r[ax, pos_g(ax)] = meta_s[ax, pos_g(ax)]
-    wbuf[:, wrows(mine), :] = shard_ref[...]
 
     pl.semaphore_wait(barrier, 2 * (SIDE - 1) + n_role)
 
@@ -208,7 +186,6 @@
         for ax in (0, 1):
             meta_copy(ax, j).start()
 
-    each(1, SIDE, meta_start)
     for kind in (0, 1):
         for ax in (0, 1):
             for way in (0, 1):
@@ -224,22 +201,48 @@
 
     for i in range(1, n_role):
         w_role(i).start()
+
+    row = iota((toks, toks), 0)
+    lane = iota((toks, toks), 1)
+    same = jnp.where(lane >= per_image, 1, 0) == jnp.where(row >= per_image, 1, 0)
+    before = jnp.where(same & (row < lane), 1.0, 0.0).astype(BF16)
+    experts = SIDE * SIDE
+    expert_row = iota((experts, toks), 0)
+    first_slot = jnp.where(iota((experts, toks), 1) >= per_image, float(CAP), 0.0)
+    for ax in (0, 1):
+        hit = jnp.zeros((experts, toks), F32)
+        gate = jnp.zeros((experts, toks), F32)
+        for k in range(ids_ref.shape[0]):
+            named = jnp.concatenate([ids_ref[k, i : i + 1, :] for i in range(images)], axis=1)
+            weight = jnp.concatenate([gate_ref[k, i : i + 1, :] for i in range(images)], axis=1)
+            if ax == 1:
+                named = (named & (SIDE - 1)) * SIDE + (named >> 3)
+            at = named == expert_row
+            hit = jnp.where(at, 1.0, hit)
+            gate = jnp.where(at, weight, gate)
+        place = jnp.where(hit > 0.5, mm(hit.astype(BF16), before) + first_slot, -1000.0)
+        for i in range(SIDE):
+            meta_s[ax, i, 0:SIDE, :] = place[i * SIDE : (i + 1) * SIDE]
+            meta_s[ax, i, SIDE : 2 * SIDE, :] = gate[i * SIDE : (i + 1) * SIDE]
+        meta_r[ax, pos_g(ax)] = meta_s[ax, pos_g(ax)]
+    each(1, SIDE, meta_start)
+    wbuf[:, wrows(mine), :] = shard_ref[...]
     w_core(0).start()
 
-    def forward(hop):
-        for kind in (0, 1):
-            for ax in (0, 1):
-                for way in (0, 1):
-                    if hop <= 4 - way:
-                        gath_wait(kind, ax, way, hop)
-                        if hop + 1 <= 4 - way:
-                            gath_hop(kind, ax, way, hop + 1).start()
+    def forward(kind, hop):
+        for ax in (0, 1):
+            for way in (0, 1):
+                if hop <= 4 - way:
+                    gath_wait(kind, ax, way, hop)
+                    if hop + 1 <= 4 - way:
+                        gath_hop(kind, ax, way, hop + 1).start()
 
     def meta_wait(j):
         for ax in (0, 1):
             slot = meta_r.at[ax, ring(pos_g(ax) - j)]
             copy(slot, slot, meta_sem, (ax, j - 1), dev_g(ax, ring(pos_g(ax) + j))).wait_recv()
 
+    forward(0, 1)
     each(1, SIDE, meta_wait)
     gain = drift_gain / noise_gain
     lane1 = iota((1, toks), 1)
@@ -270,38 +273,51 @@
         each(0, SIDE, turn)
 
     build(0)
-    forward(1)
+    forward(1, 1)
+    forward(0, 2)
     build(1)
-    forward(2)
+    forward(1, 2)
+    forward(0, 3)
     r_iota = iota((total, 1), 0)
     outer = lax.div(r_iota, blk)
     inner = lax.div(r_iota - outer * blk, slots)
     target = inner * blk + outer * slots + (r_iota - outer * blk - inner * slots)
     perm[...] = jnp.where(iota((total, total), 1) == target, 1.0, 0.0).astype(BF16)
-    forward(3)
+    forward(1, 3)
     for i in range(1, n_role):
         q = role_at(-i) * n_dp + dp
         block = wbuf.at[:, wrows(q), :]
         copy(block, block, wx_sem, (i - 1,), {"role": role_at(i)}).wait_recv()
         w_core(i).start()
-    forward(4)
-
-    def x_copy(buf, dst, sems, ax, j):
+    forward(0, 4)
+
+    everything = (0, half)
+
+    def x_copy(buf, dst, sems, ax, j, pre=(), cols=everything):
         to = ring(pos_x(ax) + j)
-        return copy(buf.at[ax, brows(to), :], dst.at[ax, brows(pos_x(ax)), :], sems, (ax, j - 1), dev_x(ax, to))
-
-    def x_wait(dst, sems):
+        lanes = slice(*cols)
+        return copy(
+            buf.at[ax, brows(to), lanes], dst.at[ax, brows(pos_x(ax)), lanes], sems, pre + (ax, j - 1), dev_x(ax, to)
+        )
+
+    def x_wait(dst, sems, pre=(), cols=everything, low=1, high=SIDE):
         def one(j):
             for ax in (0, 1):
-                block = dst.at[ax, brows(ring(pos_x(ax) - j)), :]
-                copy(block, block, sems, (ax, j - 1), dev_x(ax, ring(pos_x(ax) + j))).wait_recv()
-
-        each(1, SIDE, one)
-
-    def x_sent(buf, dst, sems):
+                block = dst.at[ax, brows(ring(pos_x(ax) - j)), slice(*cols)]
+                copy(block, block, sems, pre + (ax, j - 1), dev_x(ax, ring(pos_x(ax) + j))).wait_recv()
+
+        each(low, high, one)
+
+    def x_sent(buf, dst, sems, pre=(), cols=everything):
         def one(j):
             for ax in (0, 1):
-                x_copy(buf, dst, sems, ax, j).wait_send()
+                x_copy(buf, dst, sems, ax, j, pre, cols).wait_send()
+
+        each(1, SIDE, one)
+
+    def far_first(body):
+        def one(i):
+            body(SIDE // 2 + (2 * lax.rem(i, 2) - 1) * lax.div(i, 2))
 
         each(1, SIDE, one)
 
@@ -317,7 +333,7 @@
 
         each(0, 2, one)
 
-    each(1, SIDE, pack_l)
+    far_first(pack_l)
 
     def own_l(ax):
         here = pos_x(ax)
@@ -333,16 +349,17 @@
 
         each(0, 2, one)
 
+    forward(1, 4)
     each(0, SIDE, pack_n)
     for ax in (0, 1):
         recv_n[ax, brows(pos_x(ax)), :] = send_b[ax, brows(pos_x(ax)), :]
+
+    def start_n(j):
+        for ax in (0, 1):
+            x_copy(send_b, recv_n, n_sem, ax, j).start()
+
+    far_first(start_n)
     x_wait(recv_l, l_sem)
-
-    def start_n(j):
-        for ax in (0, 1):
-            x_copy(send_b, recv_n, n_sem, ax, j).start()
-
-    each(1, SIDE, start_n)
 
     for i in range(n_role):
         q = role_at(-i) * n_dp + other
@@ -372,19 +389,23 @@
     each(0, hidden_units // chunk, up)
     down_gain = 1.0 / math.sqrt(hidden_units)
 
+    parts = ((0, chunk), (chunk, half))
+
+    for part, cols in enumerate(parts):
+        for ax in (0, 1):
+            source = hid if ax == 0 else hidp
+
+            def down(n, ax=ax, source=source):
+                lanes = pl.ds(pl.multiple_of(ax * half + n * chunk, chunk), chunk)
+                send_a[ax, :, cols_at(n)] = (mm(source[...], wbuf[1, :, lanes]) * down_gain).astype(BF16)
+
+            each(cols[0] // chunk, cols[1] // chunk, down)
+
+            def start_o(j, ax=ax, part=part, cols=cols):
+                x_copy(send_a, recv_o, o_sem, ax, j, (part,), cols).start()
+
+            far_first(start_o)
     for ax in (0, 1):
-        source = hid if ax == 0 else hidp
-
-        def down(n, ax=ax, source=source):
-            cols = pl.ds(pl.multiple_of(ax * half + n * chunk, chunk), chunk)
-            send_a[ax, :, cols_at(n)] = (mm(source[...], wbuf[1, :, cols]) * down_gain).astype(BF16)
-
-        each(0, half // chunk, down)
-
-        def start_o(j, ax=ax):
-            x_copy(send_a, recv_o, o_sem, ax, j).start()
-
-        each(1, SIDE, start_o)
         recv_o[ax, brows(pos_x(ax)), :] = send_a[ax, brows(pos_x(ax)), :]
 
     x_wait(recv_n, n_sem)
@@ -405,61 +426,87 @@
 
     for i in range(n_role):
         g_core(i).start()
-    x_sent(send_b, recv_n, n_sem)
-
-    def weighed(ax, to):
-        return mm(selgt[ax, to], recv_o[ax])
+
+    def g_role(i):
+        return copy(gsend.at[i - 1], grecv.at[i - 1], gr_sem, (i - 1,), {"role": role_at(i)})
+
+    for i in range(n_role):
+        copy(gx.at[i], gx.at[i], gc_sem, (i,), {"dp": other}).wait_recv()
+    for i in range(1, n_role):
+        to = role_at(i)
+        gsend[i - 1] = (term[wrows(to * n_dp + dp), :].astype(F32) + gx[to].astype(F32)).astype(BF16)
+        g_role(i).start()
+
+    def weighed(part, ax, to):
+        return mm(selgt[ax, to], recv_o[ax, :, slice(*parts[part])])
 
     def red_slot(way, k):
         return way * 4 + k - 1
 
-    def red_copy(ax, way, k):
+    def red_copy(part, ax, way, k):
         step = d1 * (1 - 2 * way)
         slot = red_slot(way, k)
+        lanes = slice(*parts[part])
         return copy(
-            send_b.at[ax, trows(slot), :],
-            red_r.at[ax, trows(slot), :],
+            send_b.at[ax, trows(slot), lanes],
+            red_r.at[ax, trows(slot), lanes],
             red_sem,
-            (ax, slot),
+            (part, ax, slot),
             dev_g(ax, ring(pos_g(ax) + step)),
         )
 
-    def red_arrived(ax, way, k):
+    def red_arrived(part, ax, way, k):
         slot = red_slot(way, k)
-        block = red_r.at[ax, trows(slot), :]
-        copy(block, block, red_sem, (ax, slot), dev_g(ax, ring(pos_g(ax) + d1 * (1 - 2 * way)))).wait_recv()
-        return red_r[ax, trows(slot), :].astype(F32)
-
-    def reduce_step(k):
+        lanes = slice(*parts[part])
+        block = red_r.at[ax, trows(slot), lanes]
+        to = dev_g(ax, ring(pos_g(ax) + d1 * (1 - 2 * way)))
+        copy(block, block, red_sem, (part, ax, slot), to).wait_recv()
+        return red_r[ax, trows(slot), lanes].astype(F32)
+
+    def prepare(part, k):
         def one(ax):
             for way in (0, 1):
                 hops = 4 - way
-                if k > hops:
+                if k > hops and not (k == 5 and way == 0):
                     continue
                 step = d1 * (1 - 2 * way)
-                value = weighed(ax, ring(pos_g(ax) + step * (hops + 1 - k)))
+                vel[ax, way, :, slice(*parts[part])] = weighed(part, ax, ring(pos_g(ax) + step * (hops + 1 - k)))
+
+        each(0, 2, one)
+
+    def push(part, k):
+        lanes = slice(*parts[part])
+
+        def one(ax):
+            for way in (0, 1):
+                if k > 4 - way:
+                    continue
+                value = vel[ax, way, :, lanes]
                 if k > 1:
-                    value = value + red_arrived(ax, way, k - 1)
-                send_b[ax, trows(red_slot(way, k)), :] = value.astype(BF16)
-                red_copy(ax, way, k).start()
+                    value = value + red_arrived(part, ax, way, k - 1)
+                send_b[ax, trows(red_slot(way, k)), lanes] = value.astype(BF16)
+                red_copy(part, ax, way, k).start()
 
         each(0, 2, one)
-
-    x_wait(recv_o, o_sem)
-    reduce_step(1)
-
-    def g_role(i):
-        return copy(gsend.at[i - 1], grecv.at[i - 1], gr_sem, (i - 1,), {"role": role_at(i)})
-
-    for i in range(n_role):
-        copy(gx.at[i], gx.at[i], gc_sem, (i,), {"dp": other}).wait_recv()
-    for i in range(1, n_role):
-        to = role_at(i)
-        gsend[i - 1] = (term[wrows(to * n_dp + dp), :].astype(F32) + gx[to].astype(F32)).astype(BF16)
-        g_role(i).start()
-
-    reduce_step(2)
-    reduce_step(3)
+        prepare(part, k + 1)
+
+    def finish(part):
+        low, high = parts[part]
+        for ax in (0, 1):
+            cols = slice(ax * half + low, ax * half + high)
+            velocity = vel[ax, 0, :, low:high] + red_arrived(part, ax, 1, 3) + red_arrived(part, ax, 0, 4)
+            moved = (
+                keep_gain * lat_ref[:, cols].astype(F32)
+                + drift_gain * velocity
+                + noise_gain * noise_ref[:, cols].astype(F32)
+            )
+            fin_ref[:, cols] = moved.astype(BF16)
+
+    x_wait(recv_o, o_sem, (0,), parts[0])
+    x_sent(send_b, recv_n, n_sem)
+    prepare(0, 1)
+    push(0, 1)
+    push(0, 2)
 
     for i in range(1, n_role):
         copy(grecv.at[i - 1], grecv.at[i - 1], gr_sem, (i - 1,), {"role": role_at(i)}).wait_recv()
@@ -480,22 +527,22 @@
         d_role(i).start()
     d_core(0).start()
 
-    reduce_step(4)
+    push(0, 3)
+    x_wait(recv_o, o_sem, (1,), parts[1])
+    prepare(1, 1)
+    push(1, 1)
+    push(0, 4)
+    push(1, 2)
 
     for i in range(1, n_role):
         block = nd_ref.at[wrows(role_at(-i) * n_dp + dp), :]
         copy(block, block, dx_sem, (i - 1,), {"role": role_at(i)}).wait_recv()
         d_core(i).start()
 
-    for ax in (0, 1):
-        cols = slice(ax * half, (ax + 1) * half)
-        velocity = weighed(ax, pos_g(ax)) + red_arrived(ax, 1, 3) + red_arrived(ax, 0, 4)
-        moved = (
-            keep_gain * lat_ref[:, cols].astype(F32)
-            + drift_gain * velocity
-            + noise_gain * noise_ref[:, cols].astype(F32)
-        )
-        fin_ref[:, cols] = moved.astype(BF16)
+    push(1, 3)
+    push(1, 4)
+    finish(0)
+    finish(1)
 
     for i in range(n_role):
         block = nd_ref.at[wrows(role_at(-i) * n_dp + other), :]
@@ -511,11 +558,13 @@
             for way in (0, 1):
                 for hop in range(1, 5 - way):
                     gath_hop(kind, ax, way, hop).wait_send()
-    x_sent(send_a, recv_o, o_sem)
-    for ax in (0, 1):
-        for way in (0, 1):
-            for k in range(1, 5 - way):
-                red_copy(ax, way, k).wait_send()
+    for part, cols in enumerate(parts):
+        x_sent(send_a, recv_o, o_sem, (part,), cols)
+    for part in range(len(parts)):
+        for ax in (0, 1):
+            for way in (0, 1):
+                for k in range(1, 5 - way):
+                    red_copy(part, ax, way, k).wait_send()
     for i in range(1, n_role):
         w_role(i).wait_send()
         g_role(i).wait_send()
@@ -544,8 +593,8 @@
     fin, new_down = pl.pallas_call(
         functools.partial(kernel, (images, n_role, n_dp, rate)),
         out_shape=(
-            jax.ShapeDtypeStruct((toks, width), BF16),
-            jax.ShapeDtypeStruct((hidden_units, width), BF16),
+            pltpu.VMEM((toks, width), BF16),
+            pltpu.VMEM((hidden_units, width), BF16),
         ),
         in_specs=[vmem, vmem, pl.BlockSpec(memory_space=pltpu.SMEM), vmem, vmem, vmem],
         out_specs=(vmem, vmem),
@@ -571,12 +620,13 @@
             pltpu.VMEM((n_role - 1, rows, width), BF16),
             pltpu.VMEM((n_role - 1, rows, width), BF16),
             pltpu.VMEM((2, 7 * toks, half), BF16),
+            pltpu.VMEM((2, 2, toks, half), F32),
             dma((2, 2, SIDE - 1)),
             dma((2, 2, 2, 2, 4)),
             dma((2, 2, SIDE - 1)),
             dma((2, 2, SIDE - 1)),
-            dma((2, 2, SIDE - 1)),
-            dma((2, 2, 7)),
+            dma((2, 2, 2, SIDE - 1)),
+            dma((2, 2, 2, 7)),
             dma((2, n_role - 1)),
             dma((2, n_role)),
             dma((2, n_role)),
@@ -585,11 +635,11 @@
             dma((2, n_role)),
         ],
         compiler_params=pltpu.CompilerParams(
-            collective_id=0, has_side_effects=True, vmem_limit_bytes=60 * 1024 * 1024
+            collective_id=0, has_side_effects=True, vmem_limit_bytes=56 * 1024 * 1024
         ),
     )(
-        expert_ids.reshape(toks, top),
-        gate_values.reshape(toks, top),
+        jnp.transpose(expert_ids[0], (2, 0, 1)),
+        jnp.transpose(gate_values[0], (2, 0, 1)),
         advantages,
         latents.reshape(toks, width),
         noise.reshape(toks, width),

time: 191 us -> 172 us (0.901); the launches traced: 191 us -> 169 us
  Pallas kernels: 183 us -> 166 us
  local copies, waits for them, and re-layouts: 7.84 us -> 2.15 us
    pallas_call x1, Pallas kernels: 183 us -> 166 us  [per_device(): pl.pallas_call(functools.partial(kernel, (images, n_role, n_dp, rate)), o...]
    unnamed x4 -> x2, local copies, waits for them, and re-layouts: 7.84 us -> 2.15 us
where the time goes in v2:
time: 172 us; the launch traced here: 169 us
  Pallas kernels  166 us (97%)
  local copies, waits for them, and re-layouts  2.15 us (1%)
    pallas_call x1, Pallas kernels, per_device(): pl.pallas_call(functools.partial(kernel, (images, n_role, n_dp, rate)), o...  166 us

profile of v2, /device:TPU:1, one launch (start us, length us, event | category | flops | bytes accessed | tf_op | source)
XLA Modules:
  0.0 168.8 jit_solution(4691299505237300801)
XLA Ops:
  0.6 166.0 %shard_map.77 = (bf16[128,1536]{1,0:T(8,128)(2,1)S(1)}, bf16[768,1536]{1,0:T(8,128)(2,1)S(1)}) custom-call(s32[6,2,64]{2,1,0:T(2,128)} %bitcast.16, f32[6,2,64]{2,1,0:T(2,128)} %bitcast.17, f32[2]{0:T(128)} %adv_ref.1, bf16[128,1536]{1,0:T(8,128)(2,1)} %bitcast.14, bf16[128,1536]{1,0:T(8,128)(2,1)} %bitcast.15, bf16[2,96,1536]{2,1,0:T(8,128)(2,1)} %bitcast.13), custom_call_target="tpu_custom_call" | custom-call | tf_op jit(solution)/shard_map/pallas_call | solution.py:593
  166.6 0.7 copy.10
  167.4 1.4 copy.11

commit v3 on v2

--- a/solution.py
+++ b/solution.py
@@ -389,7 +389,7 @@
     each(0, hidden_units // chunk, up)
     down_gain = 1.0 / math.sqrt(hidden_units)
 
-    parts = ((0, chunk), (chunk, half))
+    parts = ((0, chunk), (chunk, 2 * chunk), (2 * chunk, half))
 
     for part, cols in enumerate(parts):
         for ax in (0, 1):
@@ -527,22 +527,29 @@
         d_role(i).start()
     d_core(0).start()
 
-    push(0, 3)
     x_wait(recv_o, o_sem, (1,), parts[1])
     prepare(1, 1)
     push(1, 1)
+    push(0, 3)
+    x_wait(recv_o, o_sem, (2,), parts[2])
+    prepare(2, 1)
+    push(2, 1)
+    push(1, 2)
     push(0, 4)
-    push(1, 2)
+    push(2, 2)
+    push(1, 3)
 
     for i in range(1, n_role):
         block = nd_ref.at[wrows(role_at(-i) * n_dp + dp), :]
         copy(block, block, dx_sem, (i - 1,), {"role": role_at(i)}).wait_recv()
         d_core(i).start()
 
-    push(1, 3)
+    push(2, 3)
     push(1, 4)
     finish(0)
+    push(2, 4)
     finish(1)
+    finish(2)
 
     for i in range(n_role):
         block = nd_ref.at[wrows(role_at(-i) * n_dp + other), :]
@@ -625,8 +632,8 @@
             dma((2, 2, 2, 2, 4)),
             dma((2, 2, SIDE - 1)),
             dma((2, 2, SIDE - 1)),
-            dma((2, 2, 2, SIDE - 1)),
-            dma((2, 2, 2, 7)),
+            dma((2, 3, 2, SIDE - 1)),
+            dma((2, 3, 2, 7)),
             dma((2, n_role - 1)),
             dma((2, n_role)),
             dma((2, n_role)),

time: 172 us -> 169 us (0.983); the launches traced: 169 us -> 168 us
  no operation moved by 1% of the time
where the time goes in v3:
time: 169 us; the launch traced here: 168 us
  Pallas kernels  165 us (98%)
  local copies, waits for them, and re-layouts  2.15 us (1%)
    pallas_call x1, Pallas kernels, per_device(): pl.pallas_call(functools.partial(kernel, (images, n_role, n_dp, rate)), o...  165 us

profile of v3, /device:TPU:1, one launch (start us, length us, event | category | flops | bytes accessed | tf_op | source)
XLA Modules:
  0.0 167.9 jit_solution(3399596548993618017)
XLA Ops:
  0.6 165.1 %shard_map.77 = (bf16[128,1536]{1,0:T(8,128)(2,1)S(1)}, bf16[768,1536]{1,0:T(8,128)(2,1)S(1)}) custom-call(s32[6,2,64]{2,1,0:T(2,128)} %bitcast.16, f32[6,2,64]{2,1,0:T(2,128)} %bitcast.17, f32[2]{0:T(128)} %adv_ref.1, bf16[128,1536]{1,0:T(8,128)(2,1)} %bitcast.14, bf16[128,1536]{1,0:T(8,128)(2,1)} %bitcast.15, bf16[2,96,1536]{2,1,0:T(8,128)(2,1)} %bitcast.13), custom_call_target="tpu_custom_call" | custom-call | tf_op jit(solution)/shard_map/pallas_call | solution.py:600
  165.7 0.7 copy.10
  166.4 1.4 copy.11

commit v4 on v3

--- a/solution.py
+++ b/solution.py
@@ -502,6 +502,28 @@
             )
             fin_ref[:, cols] = moved.astype(BF16)
 
+    def meta_sent(j):
+        for ax in (0, 1):
+            meta_copy(ax, j).wait_send()
+
+    each(1, SIDE, meta_sent)
+    for kind in (0, 1):
+        for ax in (0, 1):
+            for way in (0, 1):
+                for hop in range(1, 5 - way):
+                    gath_hop(kind, ax, way, hop).wait_send()
+    for i in range(1, n_role):
+        w_role(i).wait_send()
+    for i in range(n_role):
+        w_core(i).wait_send()
+        g_core(i).wait_send()
+
+    def reduced(part):
+        for ax in (0, 1):
+            for way in (0, 1):
+                for k in range(1, 5 - way):
+                    red_copy(part, ax, way, k).wait_send()
+
     x_wait(recv_o, o_sem, (0,), parts[0])
     x_sent(send_b, recv_n, n_sem)
     prepare(0, 1)
@@ -548,6 +570,12 @@
     push(1, 4)
     finish(0)
     push(2, 4)
+    for part, cols in enumerate(parts):
+        x_sent(send_a, recv_o, o_sem, (part,), cols)
+    for i in range(1, n_role):
+        g_role(i).wait_send()
+    reduced(0)
+    reduced(1)
     finish(1)
     finish(2)
 
@@ -555,30 +583,10 @@
         block = nd_ref.at[wrows(role_at(-i) * n_dp + other), :]
         copy(block, block, dc_sem, (i,), {"dp": other}).wait_recv()
 
-    def meta_sent(j):
-        for ax in (0, 1):
-            meta_copy(ax, j).wait_send()
-
-    each(1, SIDE, meta_sent)
-    for kind in (0, 1):
-        for ax in (0, 1):
-            for way in (0, 1):
-                for hop in range(1, 5 - way):
-                    gath_hop(kind, ax, way, hop).wait_send()
-    for part, cols in enumerate(parts):
-        x_sent(send_a, recv_o, o_sem, (part,), cols)
-    for part in range(len(parts)):
-        for ax in (0, 1):
-            for way in (0, 1):
-                for k in range(1, 5 - way):
-                    red_copy(part, ax, way, k).wait_send()
-    for i in range(1, n_role):
-        w_role(i).wait_send()
-        g_role(i).wait_send()
+    reduced(2)
+    for i in range(1, n_role):
         d_role(i).wait_send()
     for i in range(n_role):
-        w_core(i).wait_send()
-        g_core(i).wait_send()
         d_core(i).wait_send()
 
 

time: 169 us -> 169 us (level)
  no operation moved by 1% of the time
where the time goes in v4:
time: 169 us; the launch traced here: 168 us
  Pallas kernels  165 us (98%)
  local copies, waits for them, and re-layouts  2.15 us (1%)
    pallas_call x1, Pallas kernels, per_device(): pl.pallas_call(functools.partial(kernel, (images, n_role, n_dp, rate)), o...  165 us

profile of v4, /device:TPU:1, one launch (start us, length us, event | category | flops | bytes accessed | tf_op | source)
XLA Modules:
  0.0 167.5 jit_solution(12301436318606024557)
XLA Ops:
  0.6 164.7 %shard_map.77 = (bf16[128,1536]{1,0:T(8,128)(2,1)S(1)}, bf16[768,1536]{1,0:T(8,128)(2,1)S(1)}) custom-call(s32[6,2,64]{2,1,0:T(2,128)} %bitcast.16, f32[6,2,64]{2,1,0:T(2,128)} %bitcast.17, f32[2]{0:T(128)} %adv_ref.1, bf16[128,1536]{1,0:T(8,128)(2,1)} %bitcast.14, bf16[128,1536]{1,0:T(8,128)(2,1)} %bitcast.15, bf16[2,96,1536]{2,1,0:T(8,128)(2,1)} %bitcast.13), custom_call_target="tpu_custom_call" | custom-call | tf_op jit(solution)/shard_map/pallas_call | solution.py:608
  165.4 0.7 copy.10
  166.1 1.4 copy.11
